TPU v7x, 128 devices: a whole 4x4x4 slice. The times are simulated.
128 devices in a mesh: col: 4 (over x_hi, core), af: 32 (over z, x_lo, y).
Axes of the slice: x: 4 (x_hi: 2, x_lo: 2; x = x_hi * 2 + x_lo), y: 4, z: 4, core: 2. Of those that a mesh axis runs over, the one named last changes fastest.
Arguments:
- coarse_state: float32 [3, 8, 512, 1024], P(None, None, 'af', 'col'), may hold values from 0.1 to 2
- coarse_kappa: float32 [8, 512, 1024], P(None, 'af', 'col'), may hold values from 0.25 to 1
- coarse_rate: float32 [8, 512, 1024], P(None, 'af', 'col'), may hold values from 0.5 to 6
- fine_state: float32 [512, 3, 32, 1024], P(('col', 'af')), may hold values from 0.1 to 2
- fine_kappa: float32 [512, 32, 1024], P(('col', 'af')), may hold values from 0.25 to 1
- fine_rate: float32 [512, 32, 1024], P(('col', 'af')), may hold values from 0.5 to 6
- boxes: int32 [512, 2], replicated, may hold values from 0 to 127, as said below
- cover: int32 [64, 128], replicated, may hold values from -1 to 511, as said below
Outputs:
- coarse_out: float32 [3, 8, 512, 1024], P(None, None, 'af', 'col')
- fine_out: float32 [512, 3, 32, 1024], P(('col', 'af'))
Inputs may be any that keep to these rules, and one draw needn't show every extreme that they name: `boxes`: A patch's block spans all 8 planes; it lies in the 32 block rows of one col index, never in the first or last of them nor in the slab's first or last block column, and no two patches share a face. The patches whose blocks lie in one col index's rows are the rows of the fine arrays held by that col index, in no particular order. The 2 block columns of one af index hold at most 10 patches, and in every col index some af index holds exactly that many. cover[bx, by] is the patch whose block is (bx, by), or -1 where none is; it agrees with boxes, and every patch appears once.
All inputs are finite; a program needn't handle non-finite values.
Results may differ from a plain program's by a relative error of at most 0.0003.
Values sent between devices are 32-bit elements; how exact they have to be, the bound alone decides.
A program may use at most 192 MiB of HBM per device.

v0:
```python
import jax
import jax.numpy as jnp
from jax import lax
from jax.sharding import PartitionSpec as P

NZC = 8
RATIO = 4
BLK = 8
DT_COARSE = 1.0 / 28.0
DIFFUSE = (1.0, 0.7, 0.45)
NEIGHBOURS = ((1, 0, 0), (-1, 0, 0), (0, 1, 0), (0, -1, 0), (0, 0, 1), (0, 0, -1))


def with_halo(cells, sides, width):
    for axis, dim in sides:
        count = lax.axis_size(axis)
        ends = count - 1
        head = lax.slice_in_dim(cells, 0, width, axis=dim)
        tail = lax.slice_in_dim(cells, cells.shape[dim] - width, cells.shape[dim], axis=dim)
        cells = jnp.concatenate(
            [
                lax.ppermute(tail, axis, [(i, (i + 1) % count) for i in range(ends)]),
                cells,
                lax.ppermute(head, axis, [((i + 1) % count, i) for i in range(ends)]),
            ],
            axis=dim,
        )
    return cells


def harmonic(first, second):
    summed = first + second
    positive = summed > 0.0
    return jnp.where(positive, 2.0 * first * second / jnp.where(positive, summed, 1.0), 0.0)


def combine(center, conduct, neighbour_list, reaction, inv_square, step_size):
    summed = jnp.zeros_like(center)
    for values, coeffs in neighbour_list:
        summed = summed + harmonic(conduct, coeffs) * (values - center)
    spread = (
        jnp.stack([DIFFUSE[0] * summed[0], DIFFUSE[1] * summed[1], DIFFUSE[2] * summed[2]])
        * inv_square
    )
    forward = reaction * (center[0] * center[1] - center[2])
    change = spread + jnp.stack([-forward, -forward, forward])
    return center + step_size * change


def window(values, step_z, step_x, step_y):
    depth_len = values.shape[-3] - 2
    across = values.shape[-2] - 2
    along_len = values.shape[-1] - 2
    return values[
        ...,
        1 + step_z : 1 + step_z + depth_len,
        1 + step_x : 1 + step_x + across,
        1 + step_y : 1 + step_y + along_len,
    ]


def coarse_advance(padded_xy, conduct_xy, reaction):
    padded = jnp.pad(padded_xy, ((0, 0), (1, 1), (0, 0), (0, 0)))
    conduct = jnp.pad(conduct_xy, ((1, 1), (0, 0), (0, 0)))
    neighbour_list = [
        (
            window(padded, offsets[0], offsets[1], offsets[2]),
            window(conduct, offsets[0], offsets[1], offsets[2]),
        )
        for offsets in NEIGHBOURS
    ]
    return combine(
        window(padded, 0, 0, 0), window(conduct, 0, 0, 0), neighbour_list, reaction, 1.0, DT_COARSE
    )


def upsample(strips):
    return jnp.repeat(jnp.repeat(strips, RATIO, axis=-2), RATIO, axis=-1)


def patch_step(fields, conduct, reaction, strips):
    ghosts = upsample(strips)
    edge_len = ghosts.shape[-1]
    position = lax.broadcasted_iota(jnp.int32, (1, edge_len * edge_len), 1)
    column = position % edge_len
    row_pos = position // edge_len
    zero_fields = jnp.zeros_like(fields[:, :1])
    zero_conduct = jnp.zeros_like(conduct[:1])
    upward = (
        jnp.concatenate([fields[:, 1:], zero_fields], axis=1),
        jnp.concatenate([conduct[1:], zero_conduct], axis=0),
    )
    downward = (
        jnp.concatenate([zero_fields, fields[:, :-1]], axis=1),
        jnp.concatenate([zero_conduct, conduct[:-1]], axis=0),
    )
    last_row = row_pos == edge_len - 1
    first_row = row_pos == 0
    last_col = column == edge_len - 1
    first_col = column == 0
    next_x = (
        jnp.where(
            last_row, jnp.tile(ghosts[1], (1, 1, edge_len)), jnp.roll(fields, -edge_len, axis=-1)
        ),
        jnp.where(last_row, conduct, jnp.roll(conduct, -edge_len, axis=-1)),
    )
    prev_x = (
        jnp.where(
            first_row, jnp.tile(ghosts[0], (1, 1, edge_len)), jnp.roll(fields, edge_len, axis=-1)
        ),
        jnp.where(first_row, conduct, jnp.roll(conduct, edge_len, axis=-1)),
    )
    next_y = (
        jnp.where(
            last_col, jnp.repeat(ghosts[3], edge_len, axis=-1), jnp.roll(fields, -1, axis=-1)
        ),
        jnp.where(last_col, conduct, jnp.roll(conduct, -1, axis=-1)),
    )
    prev_y = (
        jnp.where(
            first_col, jnp.repeat(ghosts[2], edge_len, axis=-1), jnp.roll(fields, 1, axis=-1)
        ),
        jnp.where(first_col, conduct, jnp.roll(conduct, 1, axis=-1)),
    )
    return combine(
        fields,
        conduct,
        [upward, downward, next_x, prev_x, next_y, prev_y],
        reaction,
        float(RATIO * RATIO),
        DT_COARSE / RATIO,
    )


def restrict(fields):
    shaped = fields.reshape(3, NZC, RATIO, BLK, RATIO, BLK, RATIO)
    return jnp.mean(shaped, axis=(2, 4, 6)).reshape(-1)


def rim_rows(outer, block_cols, block_rows):
    species, planes, reach_x, cells_y = outer.shape
    padded_y = jnp.pad(outer, ((0, 0), (0, 0), (0, 0), (1, 1)))
    collected = []
    for column in range(block_cols):
        base_x = BLK * column
        lower_x = (
            outer[:, :, base_x, :].reshape(species, planes, block_rows, BLK).transpose(2, 0, 1, 3)
        )
        upper_x = (
            outer[:, :, base_x + BLK + 1, :]
            .reshape(species, planes, block_rows, BLK)
            .transpose(2, 0, 1, 3)
        )
        lower_y = padded_y[:, :, base_x + 1 : base_x + 1 + BLK, 0:cells_y:BLK].transpose(3, 0, 1, 2)
        upper_y = padded_y[
            :, :, base_x + 1 : base_x + 1 + BLK, BLK + 1 : cells_y + 2 : BLK
        ].transpose(3, 0, 1, 2)
        face_rows = jnp.stack([lower_x, upper_x, lower_y, upper_y], axis=1)
        collected.append(face_rows.reshape(block_rows, -1))
    return jnp.concatenate(collected, axis=0)


def sum_sources(received):
    return jnp.sum(received, axis=0)


def per_device(
    coarse_state, coarse_kappa, coarse_rate, fine_state, fine_kappa, fine_rate, boxes, cover
):
    af_count = lax.axis_size("af")
    af_index = lax.axis_index("af")
    col_index = lax.axis_index("col")
    slot_count = fine_state.shape[0]
    cells_x = coarse_state.shape[2]
    cells_y = coarse_state.shape[3]
    block_cols = cells_x // BLK
    block_rows = cells_y // BLK
    group_size = af_count * slot_count
    group_base = col_index * group_size
    stacked = jnp.concatenate([coarse_state, coarse_kappa[None]], axis=0)
    widened = with_halo(stacked, (("col", 3), ("af", 2)), 1)
    coarse_new = coarse_advance(widened[:3], widened[3], coarse_rate)
    outer_new = with_halo(coarse_new, (("af", 2),), 1)
    outer_old = widened[:3, :, :, 1:-1]
    group_boxes = lax.dynamic_slice_in_dim(boxes, group_base, group_size, 0)
    local_x = group_boxes[:, 0] - af_index * block_cols
    local_y = group_boxes[:, 1] - col_index * block_rows
    inside = (local_x >= 0) & (local_x < block_cols) & (local_y >= 0) & (local_y < block_rows)
    block_ids = jnp.where(inside, local_x * block_rows + local_y, -1)
    targets = (
        block_ids[:, None] == jnp.arange(block_cols * block_rows, dtype=jnp.int32)[None, :]
    ).astype(jnp.float32)
    earlier = rim_rows(outer_old, block_cols, block_rows)
    updated = rim_rows(outer_new, block_cols, block_rows)
    fields = fine_state
    for substep in range(RATIO):
        fraction = substep / RATIO
        current = earlier + fraction * (updated - earlier)
        send_rows = jnp.dot(targets, current, precision=lax.Precision.HIGHEST)
        strips = sum_sources(
            lax.all_to_all(
                send_rows.reshape(af_count, slot_count, current.shape[1]),
                "af",
                split_axis=0,
                concat_axis=0,
                tiled=True,
            )
        )
        strips = strips.reshape(slot_count, 4, 3, NZC, BLK)
        fields = jax.vmap(patch_step)(fields, fine_kappa, fine_rate, strips)
    averages = jax.vmap(restrict)(fields)
    cover_mine = lax.dynamic_slice(
        cover, (af_index * block_cols, col_index * block_rows), (block_cols, block_rows)
    ).reshape(-1)
    wanted = cover_mine - group_base
    portion = lax.all_gather(averages, "af", axis=0, tiled=True)
    selector = (wanted[:, None] == jnp.arange(portion.shape[0], dtype=jnp.int32)[None, :]).astype(
        jnp.float32
    )
    placed = jnp.dot(selector, portion, precision=lax.Precision.HIGHEST)
    placed = (
        placed.reshape(block_cols, block_rows, 3, NZC, BLK, BLK)
        .transpose(2, 3, 0, 4, 1, 5)
        .reshape(3, NZC, cells_x, cells_y)
    )
    covered = (cover_mine >= 0).reshape(block_cols, block_rows)
    covered = jnp.repeat(jnp.repeat(covered, BLK, axis=0), BLK, axis=1)
    coarse_out = jnp.where(covered[None, None], placed, coarse_new)
    return (coarse_out, fields)


def solution(mesh):
    return jax.shard_map(
        per_device,
        mesh=mesh,
        in_specs=(
            P(None, None, "af", "col"),
            P(None, "af", "col"),
            P(None, "af", "col"),
            P(("col", "af"), None, None, None),
            P(("col", "af"), None, None),
            P(("col", "af"), None, None),
            P(),
            P(),
        ),
        out_specs=(P(None, None, "af", "col"), P(("col", "af"), None, None, None)),
        check_vma=False,
    )
```

profile of v0, /device:TPU:4, one launch (start us, length us, event | category | flops | bytes accessed | tf_op | source)
XLA Modules:
  0.0 597.3 jit_solution(5692772814283135084)
XLA Ops:
  4.6 5.1 collective-permute-start.1
  31.8 4.5 compare_select_fusion.10
  46.5 3.5 collective-permute-start.2
  61.2 3.1 slice.500
  64.3 3.1 slice.503
  67.4 3.1 slice.504
  77.2 4.1 collective-permute-start.4
  104.3 3.1 slice.532
  107.4 3.1 slice.533
  124.3 12.2 %all-to-all-start = ((f32[32,4,768]{2,1,0:T(4,128)}), f32[32,4,768]{2,1,0:T(4,128)}, u32[]{:S(2)}, u32[]{:S(2)}) async-start(f32[32,4,768]{2,1,0:T(4,128)} %reshape.321), calls=%async_computation | async-start | bytes 786432 | tf_op jit(solution)/shard_map/all_to_all | solution.py:201
  146.5 8.9 %all-to-all-start.1 = ((f32[32,4,768]{2,1,0:T(4,128)}), f32[32,4,768]{2,1,0:T(4,128)}, u32[]{:S(2)}, u32[]{:S(2)}) async-start(f32[32,4,768]{2,1,0:T(4,128)} %reshape.327), calls=%async_computation.1 | async-start | bytes 786432 | tf_op jit(solution)/shard_map/all_to_all | solution.py:201
  162.3 3.7 broadcast_in_dim.329
  166.0 5.9 reshape.325
  172.0 3.7 broadcast_in_dim.332
  175.8 5.9 reshape.326
  184.8 5.9 tile.82
  193.8 6.0 %tile.85 = f32[4,3,32,1024]{3,2,0,1:T(8,128)} reshape(f32[4,3,32,32,32]{4,3,2,0,1:T(8,128)} %tile.84) | data formatting | bytes 3145728 | tf_op jit(solution)/shard_map/vmap()/tile | solution.py:109
  199.8 7.7 %fusion.5 = f32[4,3,32,1024]{3,2,0,1:T(8,128)S(1)} fusion(f32[4,3,32,1024]{3,2,0,1:T(8,128)} %tile.82, f32[4,3,32,32]{3,2,0,1:T(8,128)} %get-tuple-element.69, f32[4,3,32,992]{3,2,0,1:T(8,128)} %get-tuple-element.71, f32[4,3,32,1024]{3,2,0,1:T(8,128)} %tile.85, f32[4,3,32,992]{3,2,0,1:T(8,128)} %get-tuple-element.70, f32[4,3,32,32]{3,2,0,1:T(8,128)} %get-tuple-element.68, ...), kind=kLoop, calls=%fused_computation.8 | loop fusion | flops 9830400 | bytes 21925888 | tf_op jit(solution)/shard_map/vmap()/add | solution.py:40
  218.0 8.4 %all-to-all-start.2 = ((f32[32,4,768]{2,1,0:T(4,128)}), f32[32,4,768]{2,1,0:T(4,128)S(1)}, u32[]{:S(2)}, u32[]{:S(2)}) async-start(f32[32,4,768]{2,1,0:T(4,128)} %reshape.333), calls=%async_computation.2 | async-start | bytes 786432 | tf_op jit(solution)/shard_map/all_to_all | solution.py:201
  236.2 4.8 broadcast_in_dim.335
  241.0 5.9 reshape.331
  248.6 4.8 broadcast_in_dim.336
  253.4 5.9 reshape.332
  261.1 3.9 tile.87
  265.0 5.9 tile.88
  272.6 3.9 tile.90
  276.5 5.9 tile.91
  282.5 8.4 %fusion.21 = f32[4,3,32,1024]{3,2,0,1:T(8,128)S(1)} fusion(f32[4,3,32,1024]{3,2,0,1:T(8,128)} %tile.88, f32[4,3,32,32]{3,2,0,1:T(8,128)} %get-tuple-element.56, f32[4,3,32,992]{3,2,0,1:T(8,128)} %get-tuple-element.58, f32[4,3,32,1024]{3,2,0,1:T(8,128)} %tile.91, f32[4,3,32,992]{3,2,0,1:T(8,128)} %get-tuple-element.57, ...), kind=kLoop, calls=%fused_computation.29 | loop fusion | flops 12976128 | bytes 24547328 | tf_op jit(solution)/shard_map/vmap()/add | solution.py:40
  303.2 8.6 %all-to-all-start.3 = ((f32[32,4,768]{2,1,0:T(4,128)}), f32[32,4,768]{2,1,0:T(4,128)}, u32[]{:S(2)}, u32[]{:S(2)}) async-start(f32[32,4,768]{2,1,0:T(4,128)} %reshape.339), calls=%async_computation.3 | async-start | bytes 786432 | tf_op jit(solution)/shard_map/all_to_all | solution.py:201
  316.6 3.7 broadcast_in_dim.339
  320.4 5.9 reshape.337
  327.3 3.7 broadcast_in_dim.340
  331.0 5.9 reshape.338
  341.0 5.9 tile.94
  350.0 6.0 %tile.97 = f32[4,3,32,1024]{3,2,0,1:T(8,128)} reshape(f32[4,3,32,32,32]{4,3,2,0,1:T(8,128)} %tile.96) | data formatting | bytes 3145728 | tf_op jit(solution)/shard_map/vmap()/tile | solution.py:109
  356.1 10.2 %fusion.37 = f32[4,3,32,1024]{3,2,0,1:T(8,128)S(1)} fusion(f32[4,3,32,1024]{3,2,0,1:T(8,128)} %tile.94, f32[4,3,32,32]{3,2,0,1:T(8,128)} %get-tuple-element.43, f32[4,3,32,992]{3,2,0,1:T(8,128)} %get-tuple-element.45, f32[4,3,32,1024]{3,2,0,1:T(8,128)} %tile.97, f32[4,3,32,992]{3,2,0,1:T(8,128)} %get-tuple-element.44, ...), kind=kLoop, calls=%fused_computation.50 | loop fusion | flops 16121856 | bytes 27168768 | tf_op jit(solution)/shard_map/vmap()/add | solution.py:40
  380.6 3.7 broadcast_in_dim.343
  384.3 5.9 reshape.343
  390.3 3.7 broadcast_in_dim.344
  394.1 5.9 reshape.344
  403.1 5.9 tile.100
  412.1 6.1 %tile.103 = f32[4,3,32,1024]{3,2,0,1:T(8,128)} reshape(f32[4,3,32,32,32]{4,3,2,0,1:T(8,128)} %tile.102) | data formatting | bytes 3145728 | tf_op jit(solution)/shard_map/vmap()/tile | solution.py:109
  418.2 7.3 %fusion.50 = f32[4,3,32,1024]{3,2,0,1:T(8,128)S(1)} fusion(f32[4,3,32,1024]{3,2,0,1:T(8,128)} %tile.100, f32[4,3,32,1024]{3,2,0,1:T(8,128)} %tile.103, f32[4,3,32,1024]{3,2,0,1:T(8,128)} %reshape.343, f32[4,3,32,1024]{3,2,0,1:T(8,128)} %reshape.344, f32[4,32,1024]{2,1,0:T(8,128)} %get-tuple-element.95, f32[4,32,1024]{2,1,0:T(8,128)S(1)} %copy-done.21, ...), kind=kLoop, calls=%fused_computation.68 | loop fusion | flops 9830400 | bytes 21925888 | tf_op jit(solution)/shard_map/vmap()/add | solution.py:40
  427.1 53.4 %reshape.345 = f32[4,3,8,4,8,4,8,4]{7,6,5,4,3,2,1,0:T(8,128)} reshape(f32[4,3,32,1024]{3,2,1,0:T(8,128)S(1)} %bitcast_add_fusion) | data formatting | bytes 3145728 | tf_op jit(solution)/shard_map/vmap()/reshape | solution.py:136
  480.5 17.8 %reduce_sum.49 = f32[4,3,8,8,8]{4,3,2,1,0:T(8,128)S(1)} reduce(f32[4,3,8,4,8,4,8,4]{7,6,5,4,3,2,1,0:T(8,128)} %reshape.345, f32[]{:T(128)} %constant.94.clone.1), dimensions={3,5,7}, to_apply=%region_4.5 | reduce | flops 387072 | bytes 1597444 | tf_op jit(solution)/shard_map/vmap()/reduce_sum | solution.py:137
  498.6 85.9 %all-gather = f32[32,4,1536]{2,1,0:T(4,128)S(1)} all-gather(f32[1,4,1536]{2,1,0:T(4,128)S(1)} %reshape.348), channel_id=1, replica_groups=mesh['col'=4,'af'=32] {'af'}, dimensions={0}, use_global_device_ids=true | all-gather | bytes 811008 | tf_op jit(solution)/shard_map/all_gather | solution.py:216
  586.5 3.9 copy.314
  590.5 5.7 reshape.347
  (355 shorter events, 189.6 us)
Async XLA Ops:
  0.6 25.3 %copy-start = (s32[512,2]{0,1:T(2,128)S(1)}, s32[512,2]{0,1:T(2,128)}, u32[]{:S(2)}) copy-start(s32[512,2]{0,1:T(2,128)} %param.14) | copy-start | bytes 12292
  0.6 11.4 %copy-start.3 = (f32[4,32,1024]{2,1,0:T(8,128)S(1)}, f32[4,32,1024]{2,1,0:T(8,128)}, u32[]{:S(2)}) copy-start(f32[4,32,1024]{2,1,0:T(8,128)} %param.12) | copy-start | bytes 1572868
  2.6 41.3 %collective-permute-start = (f32[4,8,16,1]{3,2,1,0:T(8,128)}, f32[4,8,16,1]{3,2,1,0:T(8,128)}, u32[]{:S(2)}, u32[]{:S(2)}) collective-permute-start(f32[4,8,16,1]{3,2,1,0:T(8,128)} %get-tuple-element.108), channel_id=1, source_target_pairs={{0,32},{32,64},{64,96},{1,33},{33,65},{65,97},{2,34},{34,66},{66,9... | collective-permute-start | bytes 6152 | tf_op jit(solution)/shard_map/ppermute | solution.py:22
  4.6 39.4 %collective-permute-start.1 = (f32[4,8,16,1]{3,2,1,0:T(8,128)}, f32[4,8,16,1]{3,2,1,0:T(8,128)}, u32[]{:S(2)}, u32[]{:S(2)}) collective-permute-start(f32[4,8,16,1]{3,2,1,0:T(8,128)} %get-tuple-element.109), channel_id=1, source_target_pairs={{32,0},{64,32},{96,64},{33,1},{65,33},{97,65},{34,2},{66,34},{98,6... | collective-permute-start | bytes 6152 | tf_op jit(solution)/shard_map/ppermute | solution.py:24
  11.5 188.3 %copy-start.72 = (pred[1024]{0:T(1024)(128)(4,1)}, pred[1024]{0:T(1024)(128)(4,1)S(1)}, u32[]{:S(2)}) copy-start(pred[1024]{0:T(1024)(128)(4,1)S(1)} %get-tuple-element.121) | copy-start | bytes 3076
  11.5 188.3 %copy-start.75 = (pred[1024]{0:T(1024)(128)(4,1)}, pred[1024]{0:T(1024)(128)(4,1)S(1)}, u32[]{:S(2)}) copy-start(pred[1024]{0:T(1024)(128)(4,1)S(1)} %get-tuple-element.122) | copy-start | bytes 3076
  12.1 187.7 %copy-start.78 = (pred[1024]{0:T(1024)(128)(4,1)}, pred[1024]{0:T(1024)(128)(4,1)S(1)}, u32[]{:S(2)}) copy-start(pred[1024]{0:T(1024)(128)(4,1)S(1)} %get-tuple-element.123) | copy-start | bytes 3076
  27.8 328.2 %copy-start.6 = (f32[1,4,32,1024]{3,2,1,0:T(8,128)}, f32[1,4,32,1024]{3,2,1,0:T(8,128)S(1)}, u32[]{:S(2)}) copy-start(f32[1,4,32,1024]{3,2,1,0:T(8,128)S(1)} %get-tuple-element.16) | copy-start | bytes 1572868
  27.8 328.2 %copy-start.8 = (f32[4,32,1024]{2,1,0:T(8,128)}, f32[4,32,1024]{2,1,0:T(8,128)S(1)}, u32[]{:S(2)}) copy-start(f32[4,32,1024]{2,1,0:T(8,128)S(1)} %get-tuple-element.17) | copy-start | bytes 1572868
  36.3 7.6 %copy-start.47 = (f32[8,16,256]{2,1,0:T(8,128)S(1)}, f32[8,16,256]{2,1,0:T(8,128)}, u32[]{:S(2)}) copy-start(f32[8,16,256]{2,1,0:T(8,128)} %param.9) | copy-start | bytes 393220
  46.5 7.0 %collective-permute-start.2 = (f32[4,8,1,258]{3,1,2,0:T(8,128)S(1)}, f32[4,8,1,258]{3,1,2,0:T(8,128)S(1)}, u32[]{:S(2)}, u32[]{:S(2)}) collective-permute-start(f32[4,8,1,258]{3,1,2,0:T(8,128)S(1)} %get-tuple-element.89), channel_id=1, source_target_pairs={{0,1},{1,2},{2,3},{3,4},{4,5},{5,6},{6,7},{7,8},{8,9},{9,10},{10,1... | collective-permute-start | bytes 99080 | tf_op jit(solution)/shard_map/ppermute | solution.py:22
  50.0 6.0 %collective-permute-start.3 = (f32[4,8,1,258]{3,1,2,0:T(8,128)S(1)}, f32[4,8,1,258]{3,1,2,0:T(8,128)S(1)}, u32[]{:S(2)}, u32[]{:S(2)}) collective-permute-start(f32[4,8,1,258]{3,1,2,0:T(8,128)S(1)} %get-tuple-element.88), channel_id=1, source_target_pairs={{1,0},{2,1},{3,2},{4,3},{5,4},{6,5},{7,6},{8,7},{9,8},{10,9},{11,1... | collective-permute-start | bytes 99080 | tf_op jit(solution)/shard_map/ppermute | solution.py:24
  74.1 9.4 %copy-start.64 = (f32[3,8,8,32]{3,1,2,0:T(8,128)S(1)}, f32[3,8,8,32]{3,1,2,0:T(8,128)}, u32[]{:S(2)}) copy-start(f32[3,8,8,32]{3,1,2,0:T(8,128)} %slice.499) | copy-start | bytes 73732
  74.1 9.4 %copy-start.63 = (f32[3,8,8,32]{3,1,2,0:T(8,128)S(1)}, f32[3,8,8,32]{3,1,2,0:T(8,128)}, u32[]{:S(2)}) copy-start(f32[3,8,8,32]{3,1,2,0:T(8,128)} %slice.500) | copy-start | bytes 73732
  74.2 10.0 %copy-start.48 = (f32[1,8,16,256]{3,2,1,0:T(8,128)}, f32[1,8,16,256]{3,2,1,0:T(8,128)S(1)}, u32[]{:S(2)}) copy-start(f32[1,8,16,256]{3,2,1,0:T(8,128)S(1)} %copy.242) | copy-start | bytes 393220
  74.3 9.9 %copy-start.50 = (f32[1,8,16,256]{3,2,1,0:T(8,128)}, f32[1,8,16,256]{3,2,1,0:T(8,128)S(1)}, u32[]{:S(2)}) copy-start(f32[1,8,16,256]{3,2,1,0:T(8,128)S(1)} %copy.243) | copy-start | bytes 393220
  74.4 9.9 %copy-start.52 = (f32[1,8,16,256]{3,2,1,0:T(8,128)}, f32[1,8,16,256]{3,2,1,0:T(8,128)S(1)}, u32[]{:S(2)}) copy-start(f32[1,8,16,256]{3,2,1,0:T(8,128)S(1)} %copy.244) | copy-start | bytes 393220
  75.1 11.8 %copy-start.62 = (f32[3,8,8,32]{3,1,2,0:T(8,128)S(1)}, f32[3,8,8,32]{3,1,2,0:T(8,128)}, u32[]{:S(2)}) copy-start(f32[3,8,8,32]{3,1,2,0:T(8,128)} %slice.504) | copy-start | bytes 73732
  75.9 11.6 %copy-start.67 = (f32[4,8,1,258]{3,1,2,0:T(8,128)S(1)}, f32[4,8,1,258]{3,1,2,0:T(8,128)}, u32[]{:S(2)}) copy-start(f32[4,8,1,258]{3,1,2,0:T(8,128)} %copy-done.65) | copy-start | bytes 99076
  77.2 20.3 %collective-permute-start.4 = (f32[3,8,1,256]{3,1,2,0:T(8,128)}, f32[3,8,1,256]{3,1,2,0:T(8,128)}, u32[]{:S(2)}, u32[]{:S(2)}) collective-permute-start(f32[3,8,1,256]{3,1,2,0:T(8,128)} %copy.245), channel_id=1, source_target_pairs={{0,1},{1,2},{2,3},{3,4},{4,5},{5,6},{6,7},{7,8},{8,9},{9,10},{10,1... | collective-permute-start | bytes 73736 | tf_op jit(solution)/shard_map/ppermute | solution.py:22
  81.9 15.6 %collective-permute-start.5 = (f32[3,8,1,256]{3,1,2,0:T(8,128)}, f32[3,8,1,256]{3,1,2,0:T(8,128)}, u32[]{:S(2)}, u32[]{:S(2)}) collective-permute-start(f32[3,8,1,256]{3,1,2,0:T(8,128)} %copy.246), channel_id=1, source_target_pairs={{1,0},{2,1},{3,2},{4,3},{5,4},{6,5},{7,6},{8,7},{9,8},{10,9},{11,1... | collective-permute-start | bytes 73736 | tf_op jit(solution)/shard_map/ppermute | solution.py:24
  112.1 7.8 %copy-start.85 = (s32[128]{0:T(128)S(1)}, s32[128]{0:T(128)}, u32[]{:S(2)}) copy-start(s32[128]{0:T(128)} %fusion.138) | copy-start | bytes 1540
  124.3 22.2 %all-to-all-start = ((f32[32,4,768]{2,1,0:T(4,128)}), f32[32,4,768]{2,1,0:T(4,128)}, u32[]{:S(2)}, u32[]{:S(2)}) async-start(f32[32,4,768]{2,1,0:T(4,128)} %reshape.321), calls=%async_computation | async-start | bytes 786432 | tf_op jit(solution)/shard_map/all_to_all | solution.py:201
  146.5 71.5 %all-to-all-start.1 = ((f32[32,4,768]{2,1,0:T(4,128)}), f32[32,4,768]{2,1,0:T(4,128)}, u32[]{:S(2)}, u32[]{:S(2)}) async-start(f32[32,4,768]{2,1,0:T(4,128)} %reshape.327), calls=%async_computation.1 | async-start | bytes 786432 | tf_op jit(solution)/shard_map/all_to_all | solution.py:201
  193.8 6.0 %copy-start.18 = (f32[4,32,1024]{2,1,0:T(8,128)S(1)}, f32[4,32,1024]{2,1,0:T(8,128)}, u32[]{:S(2)}) copy-start(f32[4,32,1024]{2,1,0:T(8,128)} %get-tuple-element.90) | copy-start | bytes 1572868
  193.8 6.0 %copy-start.58 = (f32[4,3,32,1]{3,2,0,1:T(8,128)S(1)}, f32[4,3,32,1]{3,2,0,1:T(8,128)}, u32[]{:S(2)}) copy-start(f32[4,3,32,1]{3,2,0,1:T(8,128)} %get-tuple-element.64) | copy-start | bytes 4612
  193.8 6.0 %copy-start.59 = (f32[4,3,32,1]{3,2,0,1:T(8,128)S(1)}, f32[4,3,32,1]{3,2,0,1:T(8,128)}, u32[]{:S(2)}) copy-start(f32[4,3,32,1]{3,2,0,1:T(8,128)} %get-tuple-element.65) | copy-start | bytes 4612
  207.7 148.3 %copy-start.10 = (f32[1,4,32,1024]{3,2,1,0:T(8,128)}, f32[1,4,32,1024]{3,2,1,0:T(8,128)S(1)}, u32[]{:S(2)}) copy-start(f32[1,4,32,1024]{3,2,1,0:T(8,128)S(1)} %get-tuple-element.59) | copy-start | bytes 1572868
  218.0 85.2 %all-to-all-start.2 = ((f32[32,4,768]{2,1,0:T(4,128)}), f32[32,4,768]{2,1,0:T(4,128)S(1)}, u32[]{:S(2)}, u32[]{:S(2)}) async-start(f32[32,4,768]{2,1,0:T(4,128)} %reshape.333), calls=%async_computation.2 | async-start | bytes 786432 | tf_op jit(solution)/shard_map/all_to_all | solution.py:201
  303.2 75.3 %all-to-all-start.3 = ((f32[32,4,768]{2,1,0:T(4,128)}), f32[32,4,768]{2,1,0:T(4,128)}, u32[]{:S(2)}, u32[]{:S(2)}) async-start(f32[32,4,768]{2,1,0:T(4,128)} %reshape.339), calls=%async_computation.3 | async-start | bytes 786432 | tf_op jit(solution)/shard_map/all_to_all | solution.py:201
  350.0 6.0 %copy-start.60 = (f32[4,3,32,1]{3,2,0,1:T(8,128)S(1)}, f32[4,3,32,1]{3,2,0,1:T(8,128)}, u32[]{:S(2)}) copy-start(f32[4,3,32,1]{3,2,0,1:T(8,128)} %get-tuple-element.38) | copy-start | bytes 4612
  350.0 6.0 %copy-start.61 = (f32[4,3,32,1]{3,2,0,1:T(8,128)S(1)}, f32[4,3,32,1]{3,2,0,1:T(8,128)}, u32[]{:S(2)}) copy-start(f32[4,3,32,1]{3,2,0,1:T(8,128)} %get-tuple-element.39) | copy-start | bytes 4612
  350.0 6.0 %copy-start.77 = (pred[1024]{0:T(1024)(128)(4,1)S(1)}, pred[1024]{0:T(1024)(128)(4,1)}, u32[]{:S(2)}) copy-start(pred[1024]{0:T(1024)(128)(4,1)} %copy-done.75) | copy-start | bytes 3076
  350.0 6.0 %copy-start.80 = (pred[1024]{0:T(1024)(128)(4,1)S(1)}, pred[1024]{0:T(1024)(128)(4,1)}, u32[]{:S(2)}) copy-start(pred[1024]{0:T(1024)(128)(4,1)} %copy-done.78) | copy-start | bytes 3076
  350.0 6.0 %copy-start.83 = (pred[1024]{0:T(1024)(128)(4,1)S(1)}, pred[1024]{0:T(1024)(128)(4,1)}, u32[]{:S(2)}) copy-start(pred[1024]{0:T(1024)(128)(4,1)} %get-tuple-element.124) | copy-start | bytes 3076
  356.1 10.5 %copy-start.29 = (f32[4,32,1024]{2,1,0:T(8,128)S(1)}, f32[4,32,1024]{2,1,0:T(8,128)}, u32[]{:S(2)}) copy-start(f32[4,32,1024]{2,1,0:T(8,128)} %get-tuple-element.15) | copy-start | bytes 1572868
  356.1 10.5 %copy-start.31 = (f32[1,4,32,1024]{3,2,1,0:T(8,128)S(1)}, f32[1,4,32,1024]{3,2,1,0:T(8,128)}, u32[]{:S(2)}) copy-start(f32[1,4,32,1024]{3,2,1,0:T(8,128)} %copy-done.30) | copy-start | bytes 1572868
  356.1 10.5 %copy-start.33 = (f32[1,4,32,1024]{3,2,1,0:T(8,128)S(1)}, f32[1,4,32,1024]{3,2,1,0:T(8,128)}, u32[]{:S(2)}) copy-start(f32[1,4,32,1024]{3,2,1,0:T(8,128)} %copy-done.32) | copy-start | bytes 1572868
  356.1 10.5 %copy-start.35 = (f32[1,4,32,1024]{3,2,1,0:T(8,128)S(1)}, f32[1,4,32,1024]{3,2,1,0:T(8,128)}, u32[]{:S(2)}) copy-start(f32[1,4,32,1024]{3,2,1,0:T(8,128)} %copy-done.34) | copy-start | bytes 1572868
  356.1 10.5 %copy-start.42 = (f32[1,4,32,1024]{3,2,1,0:T(8,128)S(1)}, f32[1,4,32,1024]{3,2,1,0:T(8,128)}, u32[]{:S(2)}) copy-start(f32[1,4,32,1024]{3,2,1,0:T(8,128)} %get-tuple-element.12) | copy-start | bytes 1572868
  356.1 10.5 %copy-start.43 = (f32[4,32,1024]{2,1,0:T(8,128)S(1)}, f32[4,32,1024]{2,1,0:T(8,128)}, u32[]{:S(2)}) copy-start(f32[4,32,1024]{2,1,0:T(8,128)} %get-tuple-element.13) | copy-start | bytes 1572868
  412.1 6.1 %copy-start.19 = (f32[4,32,1024]{2,1,0:T(8,128)S(1)}, f32[4,32,1024]{2,1,0:T(8,128)}, u32[]{:S(2)}) copy-start(f32[4,32,1024]{2,1,0:T(8,128)} %get-tuple-element.90) | copy-start | bytes 1572868
  412.1 6.1 %copy-start.20 = (f32[4,32,1024]{2,1,0:T(8,128)S(1)}, f32[4,32,1024]{2,1,0:T(8,128)}, u32[]{:S(2)}) copy-start(f32[4,32,1024]{2,1,0:T(8,128)} %get-tuple-element.91) | copy-start | bytes 1572868
  412.1 6.1 %copy-start.21 = (f32[4,32,1024]{2,1,0:T(8,128)S(1)}, f32[4,32,1024]{2,1,0:T(8,128)}, u32[]{:S(2)}) copy-start(f32[4,32,1024]{2,1,0:T(8,128)} %get-tuple-element.92) | copy-start | bytes 1572868
  412.1 6.1 %copy-start.74 = (pred[1024]{0:T(1024)(128)(4,1)S(1)}, pred[1024]{0:T(1024)(128)(4,1)}, u32[]{:S(2)}) copy-start(pred[1024]{0:T(1024)(128)(4,1)} %copy-done.72) | copy-start | bytes 3076
  427.1 53.4 %copy-start.36 = (f32[4,3,32,1024]{3,2,1,0:T(8,128)}, f32[4,3,32,1024]{3,2,1,0:T(8,128)S(1)}, u32[]{:S(2)}) copy-start(f32[4,3,32,1024]{3,2,1,0:T(8,128)S(1)} %bitcast_add_fusion) | copy-start | bytes 4718596
  498.4 86.4 %copy-start.86 = (s32[64]{0:T(128)S(1)}, s32[64]{0:T(128)}, u32[]{:S(2)}) copy-start(s32[64]{0:T(128)} %sub.185) | copy-start | bytes 772
  590.4 6.7 %copy-start.1 = (s32[512,2]{0,1:T(2,128)S(1)}, s32[512,2]{0,1:T(2,128)}, u32[]{:S(2)}) copy-start(s32[512,2]{0,1:T(2,128)} %param.14) | copy-start | bytes 12292
  (49 other events, 133.1 us)
where the time goes:
time: 608 us; the launch traced here: 597 us
  local copies, waits for them, and re-layouts  357 us (59%)
  other arithmetic  87.3 us (14%)
  blocking collectives  85.9 us (14%)
  starting transfers between devices  55.6 us (9%)
  matrix products  7.74 us (1%)
    all_gather x1, blocking collectives, per_device(): portion = lax.all_gather(averages, 'af', axis=0, tiled=True)  85.9 us
    reshape x1, local copies, waits for them, and re-layouts, restrict(): shaped = fields.reshape(3, NZC, RATIO, BLK, RATIO, BLK, RATIO)  53.4 us
    another operation x12, local copies, waits for them, and re-layouts, patch_step(): jnp.tile(ghosts[1], (1, 1, edge_len))  39.5 us
    another operation x12, local copies, waits for them, and re-layouts, patch_step(): jnp.tile(ghosts[0], (1, 1, edge_len))  38.9 us
    all_to_all x4, starting transfers between devices, per_device(): lax.all_to_all(send_rows.reshape(af_count, slot_count, current.shape[1]),...  38.1 us
    add x5, other arithmetic, combine(): summed = summed + harmonic(conduct, coeffs) * (values - center)  35.9 us
    reshape x4, local copies, waits for them, and re-layouts, patch_step(): jnp.repeat(ghosts[2], edge_len, axis=-1)  23.6 us
    reshape x4, local copies, waits for them, and re-layouts, patch_step(): jnp.repeat(ghosts[3], edge_len, axis=-1)  23.6 us
  transfers between devices with their start and end apart: 10, of which 1 were waited for; matrix products, arithmetic and copies ran while one was open for 44% of the time, Pallas kernels for 0%

commit v1 on v0

--- a/solution.py
+++ b/solution.py
@@ -213,7 +213,9 @@
         cover, (af_index * block_cols, col_index * block_rows), (block_cols, block_rows)
     ).reshape(-1)
     wanted = cover_mine - group_base
-    portion = lax.all_gather(averages, "af", axis=0, tiled=True)
+    portion = jnp.concatenate(
+        lax.all_to_all(jnp.stack([averages] * lax.axis_size("af")), "af", 0, 0), axis=0
+    )
     selector = (wanted[:, None] == jnp.arange(portion.shape[0], dtype=jnp.int32)[None, :]).astype(
         jnp.float32
     )

time: 608 us -> 533 us (0.88)
  blocking collectives: 85.9 us -> 0 us
  waiting for transfers between devices: 2.21 us -> 11.5 us
  starting transfers between devices: 55.6 us -> 64 us
  local copies, waits for them, and re-layouts: 357 us -> 350 us
    all_gather x1 -> x0, blocking collectives: 85.9 us -> none  [per_device(): portion = lax.all_gather(averages, 'af', axis=0, tiled=True)]
    all_to_all x0 -> x1, waiting for transfers between devices: none -> 9.29 us  [per_device(): lax.all_to_all(jnp.stack([averages] * lax.axis_size('af')), 'af', 0, 0)]
    all_to_all x0 -> x1, starting transfers between devices: none -> 8.41 us  [per_device(): lax.all_to_all(jnp.stack([averages] * lax.axis_size('af')), 'af', 0, 0)]
  transfers between devices with their start and end apart: 10 -> 11, of which waited for: 1 -> 2; matrix products, arithmetic and copies ran while one was open for 44% -> 49% of each run, Pallas kernels for 0% -> 0%
where the time goes in v1:
time: 533 us; the launch traced here: 522 us
  local copies, waits for them, and re-layouts  350 us (66%)
  other arithmetic  86.8 us (16%)
  starting transfers between devices  64 us (12%)
  waiting for transfers between devices  11.5 us (2%)
  matrix products  7.8 us (1%)
    reshape x1, local copies, waits for them, and re-layouts, restrict(): shaped = fields.reshape(3, NZC, RATIO, BLK, RATIO, BLK, RATIO)  53.4 us
    another operation x12, local copies, waits for them, and re-layouts, patch_step(): jnp.tile(ghosts[1], (1, 1, edge_len))  39.5 us
    another operation x12, local copies, waits for them, and re-layouts, patch_step(): jnp.tile(ghosts[0], (1, 1, edge_len))  38.9 us
    all_to_all x4, starting transfers between devices, per_device(): lax.all_to_all(send_rows.reshape(af_count, slot_count, current.shape[1]),...  38.1 us
    add x5, other arithmetic, combine(): summed = summed + harmonic(conduct, coeffs) * (values - center)  36 us
    reshape x4, local copies, waits for them, and re-layouts, patch_step(): jnp.repeat(ghosts[3], edge_len, axis=-1)  23.6 us
    reshape x4, local copies, waits for them, and re-layouts, patch_step(): jnp.repeat(ghosts[2], edge_len, axis=-1)  23.6 us
    reduce_sum x1, other arithmetic, restrict(): return jnp.mean(shaped, axis=(2, 4, 6)).reshape(-1)  17.8 us
  transfers between devices with their start and end apart: 11, of which 2 were waited for; matrix products, arithmetic and copies ran while one was open for 49% of the time, Pallas kernels for 0%

profile of v1, /device:TPU:4, one launch (start us, length us, event | category | flops | bytes accessed | tf_op | source)
XLA Modules:
  0.0 522.5 jit_solution(9326713145646141320)
XLA Ops:
  4.6 5.1 collective-permute-start.1
  26.8 4.5 compare_select_fusion.10
  38.1 3.5 collective-permute-start.2
  52.8 3.1 slice.500
  58.9 3.1 slice.504
  68.8 4.1 collective-permute-start.4
  95.8 3.1 slice.532
  98.8 3.1 slice.533
  115.7 12.2 %all-to-all-start = ((f32[32,4,768]{2,1,0:T(4,128)}), f32[32,4,768]{2,1,0:T(4,128)}, u32[]{:S(2)}, u32[]{:S(2)}) async-start(f32[32,4,768]{2,1,0:T(4,128)} %reshape.376), calls=%async_computation | async-start | bytes 786432 | tf_op jit(solution)/shard_map/all_to_all | solution.py:201
  137.9 8.9 %all-to-all-start.1 = ((f32[32,4,768]{2,1,0:T(4,128)}), f32[32,4,768]{2,1,0:T(4,128)}, u32[]{:S(2)}, u32[]{:S(2)}) async-start(f32[32,4,768]{2,1,0:T(4,128)} %reshape.382), calls=%async_computation.1 | async-start | bytes 786432 | tf_op jit(solution)/shard_map/all_to_all | solution.py:201
  153.7 3.7 broadcast_in_dim.329
  157.4 5.9 %reshape.380 = f32[4,3,32,1024]{3,2,0,1:T(8,128)} reshape(f32[4,3,32,32,32]{4,3,2,0,1:T(8,128)} %broadcast_in_dim.329) | data formatting | bytes 3145728 | tf_op jit(solution)/shard_map/vmap()/reshape | solution.py:115
  163.4 3.7 broadcast_in_dim.332
  167.1 5.9 %reshape.381 = f32[4,3,32,1024]{3,2,0,1:T(8,128)} reshape(f32[4,3,32,32,32]{4,3,2,0,1:T(8,128)} %broadcast_in_dim.332) | data formatting | bytes 3145728 | tf_op jit(solution)/shard_map/vmap()/reshape | solution.py:121
  176.1 5.9 %tile.82 = f32[4,3,32,1024]{3,2,0,1:T(8,128)} reshape(f32[4,3,32,32,32]{4,3,2,0,1:T(8,128)} %tile.81) | data formatting | bytes 3145728 | tf_op jit(solution)/shard_map/vmap()/tile | solution.py:103
  185.2 6.0 %tile.85 = f32[4,3,32,1024]{3,2,0,1:T(8,128)} reshape(f32[4,3,32,32,32]{4,3,2,0,1:T(8,128)} %tile.84) | data formatting | bytes 3145728 | tf_op jit(solution)/shard_map/vmap()/tile | solution.py:109
  191.2 7.7 %fusion.5 = f32[4,3,32,1024]{3,2,0,1:T(8,128)S(1)} fusion(f32[4,3,32,1024]{3,2,0,1:T(8,128)} %tile.82, f32[4,3,32,32]{3,2,0,1:T(8,128)} %get-tuple-element.69, f32[4,3,32,992]{3,2,0,1:T(8,128)} %get-tuple-element.71, f32[4,3,32,1024]{3,2,0,1:T(8,128)} %tile.85, f32[4,3,32,992]{3,2,0,1:T(8,128)} %get-tuple-element.70, f32[4,3,32,32]{3,2,0,1:T(8,128)} %get-tuple-element.68, ...), kind=kLoop, calls=%fused_computation.8 | loop fusion | flops 9830400 | bytes 21925888 | tf_op jit(solution)/shard_map/vmap()/add | solution.py:40
  209.4 8.4 %all-to-all-start.2 = ((f32[32,4,768]{2,1,0:T(4,128)}), f32[32,4,768]{2,1,0:T(4,128)S(1)}, u32[]{:S(2)}, u32[]{:S(2)}) async-start(f32[32,4,768]{2,1,0:T(4,128)} %reshape.388), calls=%async_computation.2 | async-start | bytes 786432 | tf_op jit(solution)/shard_map/all_to_all | solution.py:201
  227.5 4.8 broadcast_in_dim.335
  232.3 5.9 %reshape.386 = f32[4,3,32,1024]{3,2,0,1:T(8,128)} reshape(f32[4,3,32,32,32]{4,3,2,0,1:T(8,128)} %broadcast_in_dim.335) | data formatting | bytes 3145728 | tf_op jit(solution)/shard_map/vmap()/reshape | solution.py:115
  239.9 4.8 broadcast_in_dim.336
  244.7 5.9 %reshape.387 = f32[4,3,32,1024]{3,2,0,1:T(8,128)} reshape(f32[4,3,32,32,32]{4,3,2,0,1:T(8,128)} %broadcast_in_dim.336) | data formatting | bytes 3145728 | tf_op jit(solution)/shard_map/vmap()/reshape | solution.py:121
  252.3 3.9 tile.87
  256.3 5.9 %tile.88 = f32[4,3,32,1024]{3,2,0,1:T(8,128)} reshape(f32[4,3,32,32,32]{4,3,2,0,1:T(8,128)} %tile.87) | data formatting | bytes 3145728 | tf_op jit(solution)/shard_map/vmap()/tile | solution.py:103
  263.9 3.9 tile.90
  267.8 5.9 %tile.91 = f32[4,3,32,1024]{3,2,0,1:T(8,128)} reshape(f32[4,3,32,32,32]{4,3,2,0,1:T(8,128)} %tile.90) | data formatting | bytes 3145728 | tf_op jit(solution)/shard_map/vmap()/tile | solution.py:109
  273.8 8.4 %fusion.21 = f32[4,3,32,1024]{3,2,0,1:T(8,128)S(1)} fusion(f32[4,3,32,1024]{3,2,0,1:T(8,128)} %tile.88, f32[4,3,32,32]{3,2,0,1:T(8,128)} %get-tuple-element.56, f32[4,3,32,992]{3,2,0,1:T(8,128)} %get-tuple-element.58, f32[4,3,32,1024]{3,2,0,1:T(8,128)} %tile.91, f32[4,3,32,992]{3,2,0,1:T(8,128)} %get-tuple-element.57, ...), kind=kLoop, calls=%fused_computation.29 | loop fusion | flops 12976128 | bytes 24547328 | tf_op jit(solution)/shard_map/vmap()/add | solution.py:40
  294.5 8.6 %all-to-all-start.3 = ((f32[32,4,768]{2,1,0:T(4,128)}), f32[32,4,768]{2,1,0:T(4,128)}, u32[]{:S(2)}, u32[]{:S(2)}) async-start(f32[32,4,768]{2,1,0:T(4,128)} %reshape.394), calls=%async_computation.3 | async-start | bytes 786432 | tf_op jit(solution)/shard_map/all_to_all | solution.py:201
  307.9 3.7 broadcast_in_dim.339
  311.6 5.9 %reshape.392 = f32[4,3,32,1024]{3,2,0,1:T(8,128)} reshape(f32[4,3,32,32,32]{4,3,2,0,1:T(8,128)} %broadcast_in_dim.339) | data formatting | bytes 3145728 | tf_op jit(solution)/shard_map/vmap()/reshape | solution.py:115
  318.5 3.7 broadcast_in_dim.340
  322.2 5.9 %reshape.393 = f32[4,3,32,1024]{3,2,0,1:T(8,128)} reshape(f32[4,3,32,32,32]{4,3,2,0,1:T(8,128)} %broadcast_in_dim.340) | data formatting | bytes 3145728 | tf_op jit(solution)/shard_map/vmap()/reshape | solution.py:121
  332.1 5.9 %tile.94 = f32[4,3,32,1024]{3,2,0,1:T(8,128)} reshape(f32[4,3,32,32,32]{4,3,2,0,1:T(8,128)} %tile.93) | data formatting | bytes 3145728 | tf_op jit(solution)/shard_map/vmap()/tile | solution.py:103
  341.2 6.0 %tile.97 = f32[4,3,32,1024]{3,2,0,1:T(8,128)} reshape(f32[4,3,32,32,32]{4,3,2,0,1:T(8,128)} %tile.96) | data formatting | bytes 3145728 | tf_op jit(solution)/shard_map/vmap()/tile | solution.py:109
  347.3 10.2 %fusion.37 = f32[4,3,32,1024]{3,2,0,1:T(8,128)S(1)} fusion(f32[4,3,32,1024]{3,2,0,1:T(8,128)} %tile.94, f32[4,3,32,32]{3,2,0,1:T(8,128)} %get-tuple-element.43, f32[4,3,32,992]{3,2,0,1:T(8,128)} %get-tuple-element.45, f32[4,3,32,1024]{3,2,0,1:T(8,128)} %tile.97, f32[4,3,32,992]{3,2,0,1:T(8,128)} %get-tuple-element.44, ...), kind=kLoop, calls=%fused_computation.50 | loop fusion | flops 16121856 | bytes 27168768 | tf_op jit(solution)/shard_map/vmap()/add | solution.py:40
  371.8 3.7 broadcast_in_dim.343
  375.5 5.9 %reshape.398 = f32[4,3,32,1024]{3,2,0,1:T(8,128)} reshape(f32[4,3,32,32,32]{4,3,2,0,1:T(8,128)} %broadcast_in_dim.343) | data formatting | bytes 3145728 | tf_op jit(solution)/shard_map/vmap()/reshape | solution.py:115
  381.5 3.7 broadcast_in_dim.344
  385.2 5.9 %reshape.399 = f32[4,3,32,1024]{3,2,0,1:T(8,128)} reshape(f32[4,3,32,32,32]{4,3,2,0,1:T(8,128)} %broadcast_in_dim.344) | data formatting | bytes 3145728 | tf_op jit(solution)/shard_map/vmap()/reshape | solution.py:121
  394.2 5.9 %tile.100 = f32[4,3,32,1024]{3,2,0,1:T(8,128)} reshape(f32[4,3,32,32,32]{4,3,2,0,1:T(8,128)} %tile.99) | data formatting | bytes 3145728 | tf_op jit(solution)/shard_map/vmap()/tile | solution.py:103
  403.2 6.1 %tile.103 = f32[4,3,32,1024]{3,2,0,1:T(8,128)} reshape(f32[4,3,32,32,32]{4,3,2,0,1:T(8,128)} %tile.102) | data formatting | bytes 3145728 | tf_op jit(solution)/shard_map/vmap()/tile | solution.py:109
  409.3 7.3 %fusion.50 = f32[4,3,32,1024]{3,2,0,1:T(8,128)S(1)} fusion(f32[4,3,32,1024]{3,2,0,1:T(8,128)} %tile.100, f32[4,3,32,1024]{3,2,0,1:T(8,128)} %tile.103, f32[4,3,32,1024]{3,2,0,1:T(8,128)} %reshape.398, f32[4,3,32,1024]{3,2,0,1:T(8,128)} %reshape.399, f32[4,32,1024]{2,1,0:T(8,128)} %get-tuple-element.95, f32[4,32,1024]{2,1,0:T(8,128)S(1)} %copy-done.21, ...), kind=kLoop, calls=%fused_computation.68 | loop fusion | flops 9830400 | bytes 21925888 | tf_op jit(solution)/shard_map/vmap()/add | solution.py:40
  418.2 53.4 %reshape.400 = f32[4,3,8,4,8,4,8,4]{7,6,5,4,3,2,1,0:T(8,128)} reshape(f32[4,3,32,1024]{3,2,1,0:T(8,128)S(1)} %bitcast_add_fusion) | data formatting | bytes 3145728 | tf_op jit(solution)/shard_map/vmap()/reshape | solution.py:136
  471.7 17.8 %reduce_sum.49 = f32[4,3,8,8,8]{4,3,2,1,0:T(8,128)S(1)} reduce(f32[4,3,8,4,8,4,8,4]{7,6,5,4,3,2,1,0:T(8,128)} %reshape.400, f32[]{:T(128)} %constant.94.clone.1), dimensions={3,5,7}, to_apply=%region_4.5 | reduce | flops 387072 | bytes 1597444 | tf_op jit(solution)/shard_map/vmap()/reduce_sum | solution.py:137
  490.7 8.4 %all-to-all-start.4 = ((f32[32,4,1536]{2,1,0:T(4,128)}), f32[32,4,1536]{2,1,0:T(4,128)S(1)}, u32[]{:S(2)}, u32[]{:S(2)}) async-start(f32[32,4,1536]{2,1,0:T(4,128)} %stack.178), calls=%async_computation.4 | async-start | bytes 1572864 | tf_op jit(solution)/shard_map/all_to_all | solution.py:217
  500.8 9.3 %all-to-all-done.4 = f32[32,4,1536]{2,1,0:T(4,128)S(1)} async-done(((f32[32,4,1536]{2,1,0:T(4,128)}), f32[32,4,1536]{2,1,0:T(4,128)S(1)}, u32[]{:S(2)}, u32[]{:S(2)}) %all-to-all-start.4) | async-done | bytes 786464 | tf_op jit(solution)/shard_map/all_to_all | solution.py:217
  511.6 4.0 copy.313
  515.6 5.7 %reshape.402 = f32[3,8,16,256]{3,2,1,0:T(8,128)S(1)} reshape(f32[3,8,2,8,32,8]{5,4,3,2,1,0:T(8,128)} %copy.313) | data formatting | bytes 786432 | tf_op jit(solution)/shard_map/reshape | solution.py:226
  (350 shorter events, 186.2 us)
Async XLA Ops:
  0.6 24.8 %copy-start = (s32[512,2]{0,1:T(2,128)S(1)}, s32[512,2]{0,1:T(2,128)}, u32[]{:S(2)}) copy-start(s32[512,2]{0,1:T(2,128)} %param.14) | copy-start | bytes 12292
  0.6 9.6 %copy-start.3 = (f32[4,32,1024]{2,1,0:T(8,128)S(1)}, f32[4,32,1024]{2,1,0:T(8,128)}, u32[]{:S(2)}) copy-start(f32[4,32,1024]{2,1,0:T(8,128)} %param.12) | copy-start | bytes 1572868
  2.6 32.9 %collective-permute-start = (f32[4,8,16,1]{3,2,1,0:T(8,128)}, f32[4,8,16,1]{3,2,1,0:T(8,128)}, u32[]{:S(2)}, u32[]{:S(2)}) collective-permute-start(f32[4,8,16,1]{3,2,1,0:T(8,128)} %get-tuple-element.108), channel_id=1, source_target_pairs={{0,32},{32,64},{64,96},{1,33},{33,65},{65,97},{2,34},{34,66},{66,9... | collective-permute-start | bytes 6152 | tf_op jit(solution)/shard_map/ppermute | solution.py:22
  4.6 31.0 %collective-permute-start.1 = (f32[4,8,16,1]{3,2,1,0:T(8,128)}, f32[4,8,16,1]{3,2,1,0:T(8,128)}, u32[]{:S(2)}, u32[]{:S(2)}) collective-permute-start(f32[4,8,16,1]{3,2,1,0:T(8,128)} %get-tuple-element.109), channel_id=1, source_target_pairs={{32,0},{64,32},{96,64},{33,1},{65,33},{97,65},{34,2},{66,34},{98,6... | collective-permute-start | bytes 6152 | tf_op jit(solution)/shard_map/ppermute | solution.py:24
  9.7 181.4 %copy-start.72 = (pred[1024]{0:T(1024)(128)(4,1)}, pred[1024]{0:T(1024)(128)(4,1)S(1)}, u32[]{:S(2)}) copy-start(pred[1024]{0:T(1024)(128)(4,1)S(1)} %get-tuple-element.121) | copy-start | bytes 3076
  9.7 181.4 %copy-start.75 = (pred[1024]{0:T(1024)(128)(4,1)}, pred[1024]{0:T(1024)(128)(4,1)S(1)}, u32[]{:S(2)}) copy-start(pred[1024]{0:T(1024)(128)(4,1)S(1)} %get-tuple-element.122) | copy-start | bytes 3076
  10.3 180.9 %copy-start.78 = (pred[1024]{0:T(1024)(128)(4,1)}, pred[1024]{0:T(1024)(128)(4,1)S(1)}, u32[]{:S(2)}) copy-start(pred[1024]{0:T(1024)(128)(4,1)S(1)} %get-tuple-element.123) | copy-start | bytes 3076
  25.4 321.8 %copy-start.6 = (f32[1,4,32,1024]{3,2,1,0:T(8,128)}, f32[1,4,32,1024]{3,2,1,0:T(8,128)S(1)}, u32[]{:S(2)}) copy-start(f32[1,4,32,1024]{3,2,1,0:T(8,128)S(1)} %get-tuple-element.16) | copy-start | bytes 1572868
  25.4 321.8 %copy-start.8 = (f32[4,32,1024]{2,1,0:T(8,128)}, f32[4,32,1024]{2,1,0:T(8,128)S(1)}, u32[]{:S(2)}) copy-start(f32[4,32,1024]{2,1,0:T(8,128)S(1)} %get-tuple-element.17) | copy-start | bytes 1572868
  38.1 7.0 %collective-permute-start.2 = (f32[4,8,1,258]{3,1,2,0:T(8,128)S(1)}, f32[4,8,1,258]{3,1,2,0:T(8,128)S(1)}, u32[]{:S(2)}, u32[]{:S(2)}) collective-permute-start(f32[4,8,1,258]{3,1,2,0:T(8,128)S(1)} %get-tuple-element.89), channel_id=1, source_target_pairs={{0,1},{1,2},{2,3},{3,4},{4,5},{5,6},{6,7},{7,8},{8,9},{9,10},{10,1... | collective-permute-start | bytes 99080 | tf_op jit(solution)/shard_map/ppermute | solution.py:22
  41.5 6.0 %collective-permute-start.3 = (f32[4,8,1,258]{3,1,2,0:T(8,128)S(1)}, f32[4,8,1,258]{3,1,2,0:T(8,128)S(1)}, u32[]{:S(2)}, u32[]{:S(2)}) collective-permute-start(f32[4,8,1,258]{3,1,2,0:T(8,128)S(1)} %get-tuple-element.88), channel_id=1, source_target_pairs={{1,0},{2,1},{3,2},{4,3},{5,4},{6,5},{7,6},{8,7},{9,8},{10,9},{11,1... | collective-permute-start | bytes 99080 | tf_op jit(solution)/shard_map/ppermute | solution.py:24
  65.6 9.4 %copy-start.64 = (f32[3,8,8,32]{3,1,2,0:T(8,128)S(1)}, f32[3,8,8,32]{3,1,2,0:T(8,128)}, u32[]{:S(2)}) copy-start(f32[3,8,8,32]{3,1,2,0:T(8,128)} %slice.499) | copy-start | bytes 73732
  65.7 9.4 %copy-start.63 = (f32[3,8,8,32]{3,1,2,0:T(8,128)S(1)}, f32[3,8,8,32]{3,1,2,0:T(8,128)}, u32[]{:S(2)}) copy-start(f32[3,8,8,32]{3,1,2,0:T(8,128)} %slice.500) | copy-start | bytes 73732
  65.8 10.0 %copy-start.48 = (f32[1,8,16,256]{3,2,1,0:T(8,128)}, f32[1,8,16,256]{3,2,1,0:T(8,128)S(1)}, u32[]{:S(2)}) copy-start(f32[1,8,16,256]{3,2,1,0:T(8,128)S(1)} %copy.241) | copy-start | bytes 393220
  65.8 9.9 %copy-start.50 = (f32[1,8,16,256]{3,2,1,0:T(8,128)}, f32[1,8,16,256]{3,2,1,0:T(8,128)S(1)}, u32[]{:S(2)}) copy-start(f32[1,8,16,256]{3,2,1,0:T(8,128)S(1)} %copy.242) | copy-start | bytes 393220
  65.9 9.8 %copy-start.52 = (f32[1,8,16,256]{3,2,1,0:T(8,128)}, f32[1,8,16,256]{3,2,1,0:T(8,128)S(1)}, u32[]{:S(2)}) copy-start(f32[1,8,16,256]{3,2,1,0:T(8,128)S(1)} %copy.243) | copy-start | bytes 393220
  66.6 11.8 %copy-start.62 = (f32[3,8,8,32]{3,1,2,0:T(8,128)S(1)}, f32[3,8,8,32]{3,1,2,0:T(8,128)}, u32[]{:S(2)}) copy-start(f32[3,8,8,32]{3,1,2,0:T(8,128)} %slice.504) | copy-start | bytes 73732
  67.4 11.6 %copy-start.67 = (f32[4,8,1,258]{3,1,2,0:T(8,128)S(1)}, f32[4,8,1,258]{3,1,2,0:T(8,128)}, u32[]{:S(2)}) copy-start(f32[4,8,1,258]{3,1,2,0:T(8,128)} %copy-done.65) | copy-start | bytes 99076
  68.8 20.2 %collective-permute-start.4 = (f32[3,8,1,256]{3,1,2,0:T(8,128)}, f32[3,8,1,256]{3,1,2,0:T(8,128)}, u32[]{:S(2)}, u32[]{:S(2)}) collective-permute-start(f32[3,8,1,256]{3,1,2,0:T(8,128)} %copy.244), channel_id=1, source_target_pairs={{0,1},{1,2},{2,3},{3,4},{4,5},{5,6},{6,7},{7,8},{8,9},{9,10},{10,1... | collective-permute-start | bytes 73736 | tf_op jit(solution)/shard_map/ppermute | solution.py:22
  73.4 15.6 %collective-permute-start.5 = (f32[3,8,1,256]{3,1,2,0:T(8,128)}, f32[3,8,1,256]{3,1,2,0:T(8,128)}, u32[]{:S(2)}, u32[]{:S(2)}) collective-permute-start(f32[3,8,1,256]{3,1,2,0:T(8,128)} %copy.245), channel_id=1, source_target_pairs={{1,0},{2,1},{3,2},{4,3},{5,4},{6,5},{7,6},{8,7},{9,8},{10,9},{11,1... | collective-permute-start | bytes 73736 | tf_op jit(solution)/shard_map/ppermute | solution.py:24
  115.7 22.2 %all-to-all-start = ((f32[32,4,768]{2,1,0:T(4,128)}), f32[32,4,768]{2,1,0:T(4,128)}, u32[]{:S(2)}, u32[]{:S(2)}) async-start(f32[32,4,768]{2,1,0:T(4,128)} %reshape.376), calls=%async_computation | async-start | bytes 786432 | tf_op jit(solution)/shard_map/all_to_all | solution.py:201
  137.9 71.4 %all-to-all-start.1 = ((f32[32,4,768]{2,1,0:T(4,128)}), f32[32,4,768]{2,1,0:T(4,128)}, u32[]{:S(2)}, u32[]{:S(2)}) async-start(f32[32,4,768]{2,1,0:T(4,128)} %reshape.382), calls=%async_computation.1 | async-start | bytes 786432 | tf_op jit(solution)/shard_map/all_to_all | solution.py:201
  185.1 6.0 %copy-start.18 = (f32[4,32,1024]{2,1,0:T(8,128)S(1)}, f32[4,32,1024]{2,1,0:T(8,128)}, u32[]{:S(2)}) copy-start(f32[4,32,1024]{2,1,0:T(8,128)} %get-tuple-element.90) | copy-start | bytes 1572868
  185.1 6.0 %copy-start.58 = (f32[4,3,32,1]{3,2,0,1:T(8,128)S(1)}, f32[4,3,32,1]{3,2,0,1:T(8,128)}, u32[]{:S(2)}) copy-start(f32[4,3,32,1]{3,2,0,1:T(8,128)} %get-tuple-element.64) | copy-start | bytes 4612
  185.2 6.1 %copy-start.59 = (f32[4,3,32,1]{3,2,0,1:T(8,128)S(1)}, f32[4,3,32,1]{3,2,0,1:T(8,128)}, u32[]{:S(2)}) copy-start(f32[4,3,32,1]{3,2,0,1:T(8,128)} %get-tuple-element.65) | copy-start | bytes 4612
  185.2 6.1 %copy-start.81 = (pred[1024]{0:T(1024)(128)(4,1)S(1)}, pred[1024]{0:T(1024)(128)(4,1)}, u32[]{:S(2)}) copy-start(pred[1024]{0:T(1024)(128)(4,1)} %get-tuple-element.124) | copy-start | bytes 3076
  199.1 148.1 %copy-start.10 = (f32[1,4,32,1024]{3,2,1,0:T(8,128)}, f32[1,4,32,1024]{3,2,1,0:T(8,128)S(1)}, u32[]{:S(2)}) copy-start(f32[1,4,32,1024]{3,2,1,0:T(8,128)S(1)} %get-tuple-element.59) | copy-start | bytes 1572868
  209.4 85.1 %all-to-all-start.2 = ((f32[32,4,768]{2,1,0:T(4,128)}), f32[32,4,768]{2,1,0:T(4,128)S(1)}, u32[]{:S(2)}, u32[]{:S(2)}) async-start(f32[32,4,768]{2,1,0:T(4,128)} %reshape.388), calls=%async_computation.2 | async-start | bytes 786432 | tf_op jit(solution)/shard_map/all_to_all | solution.py:201
  267.8 5.9 %copy-start.82 = (pred[1024]{0:T(1024)(128)(4,1)S(1)}, pred[1024]{0:T(1024)(128)(4,1)}, u32[]{:S(2)}) copy-start(pred[1024]{0:T(1024)(128)(4,1)} %get-tuple-element.124) | copy-start | bytes 3076
  294.5 75.2 %all-to-all-start.3 = ((f32[32,4,768]{2,1,0:T(4,128)}), f32[32,4,768]{2,1,0:T(4,128)}, u32[]{:S(2)}, u32[]{:S(2)}) async-start(f32[32,4,768]{2,1,0:T(4,128)} %reshape.394), calls=%async_computation.3 | async-start | bytes 786432 | tf_op jit(solution)/shard_map/all_to_all | solution.py:201
  341.2 6.0 %copy-start.60 = (f32[4,3,32,1]{3,2,0,1:T(8,128)S(1)}, f32[4,3,32,1]{3,2,0,1:T(8,128)}, u32[]{:S(2)}) copy-start(f32[4,3,32,1]{3,2,0,1:T(8,128)} %get-tuple-element.38) | copy-start | bytes 4612
  341.2 6.0 %copy-start.61 = (f32[4,3,32,1]{3,2,0,1:T(8,128)S(1)}, f32[4,3,32,1]{3,2,0,1:T(8,128)}, u32[]{:S(2)}) copy-start(f32[4,3,32,1]{3,2,0,1:T(8,128)} %get-tuple-element.39) | copy-start | bytes 4612
  341.2 6.0 %copy-start.77 = (pred[1024]{0:T(1024)(128)(4,1)S(1)}, pred[1024]{0:T(1024)(128)(4,1)}, u32[]{:S(2)}) copy-start(pred[1024]{0:T(1024)(128)(4,1)} %copy-done.75) | copy-start | bytes 3076
  341.2 6.0 %copy-start.80 = (pred[1024]{0:T(1024)(128)(4,1)S(1)}, pred[1024]{0:T(1024)(128)(4,1)}, u32[]{:S(2)}) copy-start(pred[1024]{0:T(1024)(128)(4,1)} %copy-done.78) | copy-start | bytes 3076
  341.2 6.0 %copy-start.83 = (pred[1024]{0:T(1024)(128)(4,1)S(1)}, pred[1024]{0:T(1024)(128)(4,1)}, u32[]{:S(2)}) copy-start(pred[1024]{0:T(1024)(128)(4,1)} %get-tuple-element.124) | copy-start | bytes 3076
  347.2 10.6 %copy-start.29 = (f32[4,32,1024]{2,1,0:T(8,128)S(1)}, f32[4,32,1024]{2,1,0:T(8,128)}, u32[]{:S(2)}) copy-start(f32[4,32,1024]{2,1,0:T(8,128)} %get-tuple-element.15) | copy-start | bytes 1572868
  347.2 10.6 %copy-start.31 = (f32[1,4,32,1024]{3,2,1,0:T(8,128)S(1)}, f32[1,4,32,1024]{3,2,1,0:T(8,128)}, u32[]{:S(2)}) copy-start(f32[1,4,32,1024]{3,2,1,0:T(8,128)} %copy-done.30) | copy-start | bytes 1572868
  347.2 10.6 %copy-start.33 = (f32[1,4,32,1024]{3,2,1,0:T(8,128)S(1)}, f32[1,4,32,1024]{3,2,1,0:T(8,128)}, u32[]{:S(2)}) copy-start(f32[1,4,32,1024]{3,2,1,0:T(8,128)} %copy-done.32) | copy-start | bytes 1572868
  347.2 10.6 %copy-start.35 = (f32[1,4,32,1024]{3,2,1,0:T(8,128)S(1)}, f32[1,4,32,1024]{3,2,1,0:T(8,128)}, u32[]{:S(2)}) copy-start(f32[1,4,32,1024]{3,2,1,0:T(8,128)} %copy-done.34) | copy-start | bytes 1572868
  347.3 10.6 %copy-start.42 = (f32[1,4,32,1024]{3,2,1,0:T(8,128)S(1)}, f32[1,4,32,1024]{3,2,1,0:T(8,128)}, u32[]{:S(2)}) copy-start(f32[1,4,32,1024]{3,2,1,0:T(8,128)} %get-tuple-element.12) | copy-start | bytes 1572868
  347.3 10.6 %copy-start.43 = (f32[4,32,1024]{2,1,0:T(8,128)S(1)}, f32[4,32,1024]{2,1,0:T(8,128)}, u32[]{:S(2)}) copy-start(f32[4,32,1024]{2,1,0:T(8,128)} %get-tuple-element.13) | copy-start | bytes 1572868
  403.2 6.1 %copy-start.19 = (f32[4,32,1024]{2,1,0:T(8,128)S(1)}, f32[4,32,1024]{2,1,0:T(8,128)}, u32[]{:S(2)}) copy-start(f32[4,32,1024]{2,1,0:T(8,128)} %get-tuple-element.90) | copy-start | bytes 1572868
  403.2 6.1 %copy-start.20 = (f32[4,32,1024]{2,1,0:T(8,128)S(1)}, f32[4,32,1024]{2,1,0:T(8,128)}, u32[]{:S(2)}) copy-start(f32[4,32,1024]{2,1,0:T(8,128)} %get-tuple-element.91) | copy-start | bytes 1572868
  403.2 6.1 %copy-start.21 = (f32[4,32,1024]{2,1,0:T(8,128)S(1)}, f32[4,32,1024]{2,1,0:T(8,128)}, u32[]{:S(2)}) copy-start(f32[4,32,1024]{2,1,0:T(8,128)} %get-tuple-element.92) | copy-start | bytes 1572868
  403.2 6.1 %copy-start.74 = (pred[1024]{0:T(1024)(128)(4,1)S(1)}, pred[1024]{0:T(1024)(128)(4,1)}, u32[]{:S(2)}) copy-start(pred[1024]{0:T(1024)(128)(4,1)} %copy-done.72) | copy-start | bytes 3076
  418.2 53.4 %copy-start.36 = (f32[4,3,32,1024]{3,2,1,0:T(8,128)}, f32[4,3,32,1024]{3,2,1,0:T(8,128)S(1)}, u32[]{:S(2)}) copy-start(f32[4,3,32,1024]{3,2,1,0:T(8,128)S(1)} %bitcast_add_fusion) | copy-start | bytes 4718596
  490.7 19.4 %all-to-all-start.4 = ((f32[32,4,1536]{2,1,0:T(4,128)}), f32[32,4,1536]{2,1,0:T(4,128)S(1)}, u32[]{:S(2)}, u32[]{:S(2)}) async-start(f32[32,4,1536]{2,1,0:T(4,128)} %stack.178), calls=%async_computation.4 | async-start | bytes 1572864 | tf_op jit(solution)/shard_map/all_to_all | solution.py:217
  515.6 6.7 %copy-start.1 = (s32[512,2]{0,1:T(2,128)S(1)}, s32[512,2]{0,1:T(2,128)}, u32[]{:S(2)}) copy-start(s32[512,2]{0,1:T(2,128)} %param.14) | copy-start | bytes 12292
  (47 other events, 120.1 us)
